TPU v7x, 256 devices: a whole 4x4x8 slice. The times are simulated.
256 devices in a mesh: dp: 4 (over y), seq: 8 (over z_hi, core), mp: 8 (over x, z_lo).
Axes of the slice: x: 4, y: 4, z: 8 (z_hi: 4, z_lo: 2; z = z_hi * 2 + z_lo), core: 2. Of those that a mesh axis runs over, the one named last changes fastest.
Arguments:
- queries: bfloat16 [32, 4, 32, 8192], P(('dp', 'seq'), None, None, 'mp'), may hold values from -6 to 6
- resp_kv: bfloat16 [32, 4, 32, 2, 1024], P(('dp', 'seq'), None, None, None, 'mp'), may hold values from -8 to 8
- prompt_keys: bfloat16 [4, 1024, 1024], P('dp', 'seq', 'mp'), may hold values from -6 to 6
- prompt_values: bfloat16 [4, 1024, 1024], P('dp', 'seq', 'mp'), may hold values from -6 to 6
- out_weight: bfloat16 [8192, 8192], P('mp', ('dp', 'seq')), may hold values from -3 to 3
- lengths: int32 [32, 4], replicated, may hold values from 8 to 32, as said below
- prompt_of: int32 [32, 4], replicated, may hold values from 0 to 3, each once within a row
Outputs:
- mixed: bfloat16 [4096, 8192], P(('dp', 'seq', 'mp'))
Inputs may be any that keep to these rules, and one draw needn't show every extreme that they name: `lengths`: some response has exactly 32 tokens in every draw. `prompt_of`: each source holds exactly one response to every prompt.
All inputs are finite; a program needn't handle non-finite values.
Results may differ from a plain program's by a relative error of at most 0.017.
Values may be sent and summed in bfloat16 or wider, within the bound.
A program may use at most 64 MiB of HBM per device.

v0:
```python
import math

import jax
import jax.numpy as jnp
from jax import lax
from jax.sharding import PartitionSpec as P

HD = 128


def local(queries, resp_kv, prompt_keys, prompt_values, out_weight, lengths, prompt_of):
    n_dp = lax.axis_size("dp")
    n_seq = lax.axis_size("seq")
    n_mp = lax.axis_size("mp")
    dp_idx = lax.axis_index("dp")
    seq_idx = lax.axis_index("seq")
    mp_idx = lax.axis_index("mp")
    cap = queries.shape[2]
    local_heads = queries.shape[3] // HD
    local_kv = resp_kv.shape[4] // HD
    group = local_heads // local_kv
    scale = 1.0 / math.sqrt(HD)
    source = dp_idx * n_seq + seq_idx
    own_prompts = lax.dynamic_slice_in_dim(prompt_of, source, 1, 0)[0]
    slot_order = jnp.argsort(own_prompts)
    sorted_q = jnp.take(queries, slot_order, axis=1)
    sorted_kv = jnp.take(resp_kv, slot_order, axis=1)
    arrived_q, arrived_kv = (
        lax.all_to_all(sorted_q, "dp", split_axis=1, concat_axis=1, tiled=True),
        lax.all_to_all(sorted_kv, "dp", split_axis=1, concat_axis=1, tiled=True),
    )
    matches = (prompt_of[:, :, None] == jnp.arange(n_dp, dtype=jnp.int32)[None, None, :]).astype(
        jnp.int32
    )
    by_prompt = jnp.sum(lengths[:, :, None] * matches, axis=1).reshape(n_dp, n_seq, n_dp)
    zero = jnp.zeros((), jnp.int32)
    arrived_len = lax.dynamic_slice(by_prompt, (zero, seq_idx, dp_idx), (n_dp, 1, 1)).reshape(n_dp)
    cache_k, cache_v = (
        lax.all_gather(prompt_keys, "seq", axis=1, tiled=True),
        lax.all_gather(prompt_values, "seq", axis=1, tiled=True),
    )
    prompt_len = cache_k.shape[1]
    cache_k = cache_k.reshape(prompt_len, local_kv, HD).transpose(1, 0, 2)
    cache_v = cache_v.reshape(prompt_len, local_kv, HD).transpose(1, 0, 2)
    rows = n_dp * cap
    head_queries = arrived_q.reshape(rows, local_heads, HD).transpose(1, 0, 2)
    own_k = arrived_kv[0, :, :, 0].reshape(n_dp, cap, local_kv, HD).transpose(2, 0, 1, 3)
    own_v = arrived_kv[0, :, :, 1].reshape(n_dp, cap, local_kv, HD).transpose(2, 0, 1, 3)
    positions = jnp.arange(cap, dtype=jnp.int32)
    causal = positions[:, None] >= positions[None, :]

    def head_output(head):
        kv_head = head // group
        query = lax.dynamic_index_in_dim(head_queries, head, 0, keepdims=False)
        far_k = lax.dynamic_index_in_dim(cache_k, kv_head, 0, keepdims=False)
        far_v = lax.dynamic_index_in_dim(cache_v, kv_head, 0, keepdims=False)
        near_k = lax.dynamic_index_in_dim(own_k, kv_head, 0, keepdims=False)
        near_v = lax.dynamic_index_in_dim(own_v, kv_head, 0, keepdims=False)
        far = (
            jnp.dot(query, far_k.T, preferred_element_type=jnp.float32).reshape(
                n_dp, cap, prompt_len
            )
            * scale
        )
        blocked = query.reshape(n_dp, cap, HD)
        near = (
            jnp.einsum("btd,bud->btu", blocked, near_k, preferred_element_type=jnp.float32) * scale
        )
        near = jnp.where(causal[None], near, -jnp.inf)
        top = jnp.maximum(jnp.max(far, axis=-1), jnp.max(near, axis=-1))
        far_exp = jnp.exp(far - top[..., None])
        near_exp = jnp.exp(near - top[..., None])
        total = jnp.sum(far_exp, axis=-1) + jnp.sum(near_exp, axis=-1)
        far_w = (far_exp / total[..., None]).astype(jnp.bfloat16)
        near_w = (near_exp / total[..., None]).astype(jnp.bfloat16)
        result = jnp.einsum("btn,nd->btd", far_w, far_v, preferred_element_type=jnp.float32)
        result = result + jnp.einsum(
            "btu,bud->btd", near_w, near_v, preferred_element_type=jnp.float32
        )
        return result.reshape(rows, HD)

    per_head = lax.map(head_output, jnp.arange(local_heads, dtype=jnp.int32))
    attended = per_head.transpose(1, 0, 2).reshape(rows, local_heads * HD)
    valid = (positions[None, :] < arrived_len[:, None]).reshape(rows)
    attended = jnp.where(valid[:, None], attended, 0.0).astype(jnp.bfloat16)
    share = rows // n_mp
    partial_value = jnp.dot(
        attended,
        lax.all_gather(out_weight, ("dp", "seq"), axis=1, tiled=True),
        preferred_element_type=jnp.float32,
    )
    summed = lax.psum(partial_value.astype(jnp.bfloat16), "mp").astype(jnp.float32)
    mine = lax.dynamic_slice_in_dim(summed, mp_idx * share, share, 0)
    return mine.astype(jnp.bfloat16)


def solution(mesh):
    placed = (
        P(("dp", "seq"), None, None, "mp"),
        P(("dp", "seq"), None, None, None, "mp"),
        P("dp", "seq", "mp"),
        P("dp", "seq", "mp"),
        P("mp", ("dp", "seq")),
        P(),
        P(),
    )
    return jax.shard_map(
        local, mesh=mesh, in_specs=placed, out_specs=P(("dp", "seq", "mp"), None), check_vma=False
    )
```

profile of v0, /device:TPU:8, one launch (start us, length us, event | category | flops | bytes accessed | tf_op | source)
XLA Modules:
  0.0 271.1 jit_solution(4546866035766713477)
XLA Ops:
  6.5 0.7 all-gather.2.cloned.1.call-update
  7.3 0.9 copy.34
  8.1 0.9 dynamic-slice_reduce_fusion
  9.0 0.7 sort.17
  9.8 0.6 gather_fusion.1
  10.3 0.7 fusion.13
  11.0 5.4 %all-to-all-start.1 = ((bf16[1,4,32,2,128]{4,2,3,0,1:T(8,128)(2,1)}), bf16[1,4,32,2,128]{4,2,3,0,1:T(8,128)(2,1)S(1)}, u32[]{:S(2)}, u32[]{:S(2)}) async-start(bf16[1,4,32,2,128]{4,2,3,0,1:T(8,128)(2,1)} %fusion.13), calls=%async_computation.1 | async-start | bytes 131072 | tf_op jit(solution)/shard_map/all_to_all | solution.py:30
  16.5 0.7 select_reduce_fusion
  17.3 0.6 gather_fusion
  18.0 19.6 %all_gather.9 = bf16[1,1024,128]{2,1,0:T(8,128)(2,1)S(1)} all-gather(bf16[1,128,128]{2,1,0:T(8,128)(2,1)} %param.11), channel_id=1, replica_groups=mesh['dp'=4,'seq'=8,'mp'=8] {'seq'}, dimensions={1}, use_global_device_ids=true | all-gather | bytes 294912 | tf_op jit(solution)/shard_map/all_gather | solution.py:39
  37.7 0.8 bitcast_select_fusion.1
  38.5 17.2 %all_gather.10 = bf16[1,1024,128]{2,1,0:T(8,128)(2,1)S(1)} all-gather(bf16[1,128,128]{2,1,0:T(8,128)(2,1)} %param.12), channel_id=1, replica_groups=mesh['dp'=4,'seq'=8,'mp'=8] {'seq'}, dimensions={1}, use_global_device_ids=true | all-gather | bytes 294912 | tf_op jit(solution)/shard_map/all_gather | solution.py:40
  55.7 4.8 %all-to-all-start = ((bf16[1,4,32,1024]{3,2,0,1:T(8,128)(2,1)}), bf16[1,4,32,1024]{3,2,0,1:T(8,128)(2,1)S(1)}, u32[]{:S(2)}, u32[]{:S(2)}) async-start(bf16[1,4,32,1024]{3,2,0,1:T(8,128)(2,1)} %bitcast_select_fusion.1), calls=%async_computation | async-start | bytes 524288 | tf_op jit(solution)/shard_map/all_to_all | solution.py:29
  60.5 5.8 %all-to-all-done = bf16[1,4,32,1024]{3,2,0,1:T(8,128)(2,1)S(1)} async-done(((bf16[1,4,32,1024]{3,2,0,1:T(8,128)(2,1)}), bf16[1,4,32,1024]{3,2,0,1:T(8,128)(2,1)S(1)}, u32[]{:S(2)}, u32[]{:S(2)}) %all-to-all-start) | async-done | bytes 262176 | tf_op jit(solution)/shard_map/all_to_all | solution.py:29
  66.4 32.0 %while.11 = (s32[]{:T(128)}, bf16[8,128,128]{1,2,0:T(8,128)(2,1)S(1)}, s32[8]{0:T(128)S(1)}, bf16[8,128,128]{2,1,0:T(8,128)(2,1)S(1)}, bf16[1,1024,128]{2,1,0:T(...) while((s32[]{:T(128)}, ...), condition=%wide.region_7.8_spmd.clone, body=%wide.region_2.7_spmd.clone.sunk | while | flops 70189824 | bytes 2648235 | solution.py:82
  66.4 0.6 dynamic_slice.36
  69.1 0.3 fusion.33
  69.5 0.2 fusion.35
  69.7 0.3 fusion.37
  70.4 0.6 dynamic_slice.36
  73.1 0.3 fusion.33
  73.5 0.2 fusion.35
  73.7 0.3 fusion.37
  74.4 0.6 dynamic_slice.36
  77.1 0.3 fusion.33
  77.7 0.3 fusion.37
  78.4 0.6 dynamic_slice.36
  81.1 0.3 fusion.33
  81.5 0.2 fusion.35
  81.7 0.3 fusion.37
  82.4 0.6 dynamic_slice.36
  85.1 0.3 fusion.33
  85.5 0.2 fusion.35
  85.7 0.3 fusion.37
  86.4 0.6 dynamic_slice.36
  89.1 0.3 fusion.33
  89.5 0.2 fusion.35
  89.7 0.3 fusion.37
  90.4 0.6 dynamic_slice.36
  93.1 0.3 fusion.33
  93.7 0.3 fusion.37
  94.4 0.6 dynamic_slice.36
  97.1 0.3 fusion.33
  97.7 0.3 fusion.37
  98.4 45.3 %all-gather.2.cloned.1.call-done = bf16[1024,8192]{1,0:T(8,128)(2,1)} async-done(((bf16[1024,256]{1,0:T(8,128)(2,1)}), bf16[1024,8192]{1,0:T(8,128)(2,1)}) %all-gather.2.cloned.1.call-update) | async-done | bytes 16777232 | tf_op jit(solution)/shard_map/all_gather | solution.py:89
  143.8 9.6 %convolution_convert_fusion = bf16[128,8192]{1,0:T(8,128)(2,1)} fusion(bf16[128,1024]{0,1:T(8,128)(2,1)S(1)} %fusion.12, bf16[1024,8192]{1,0:T(8,128)(2,1)} %all-gather.2.cloned.1.call-done), kind=kOutput, calls=%fused_computation.23 | convolution fusion | flops 2148532224 | bytes 19136512 | tf_op jit(solution)/shard_map/dot_general | solution.py:87
  153.4 109.2 %all-reduce.2.cloned.1.call-done = bf16[128,8192]{1,0:T(8,128)(2,1)} async-done(((bf16[128,8192]{1,0:T(8,128)(2,1)}), bf16[128,8192]{1,0:T(8,128)(2,1)}) %all-reduce.2.cloned.1.call-update) | async-done | bytes 2097168 | tf_op jit(solution)/shard_map/psum | solution.py:92
  262.6 1.7 convert_convert_fusion
  (95 shorter events, 5.7 us)
Async XLA Ops:
  6.5 10.7 %copy-start = (bf16[1,4,32,1024]{3,2,1,0:T(8,128)(2,1)S(1)}, bf16[1,4,32,1024]{3,2,1,0:T(8,128)(2,1)}, u32[]{:S(2)}) copy-start(bf16[1,4,32,1024]{3,2,1,0:T(8,128)(2,1)} %param.9) | copy-start | bytes 786436
  6.5 137.2 %all-gather.2.cloned.1.call-start = ((), (), s32[]{:S(2)}) async-start(), calls=%async_computation.2 | async-start | bytes 17301504 | tf_op jit(solution)/shard_map/all_gather | solution.py:89
  11.0 44.7 %all-to-all-start.1 = ((bf16[1,4,32,2,128]{4,2,3,0,1:T(8,128)(2,1)}), bf16[1,4,32,2,128]{4,2,3,0,1:T(8,128)(2,1)S(1)}, u32[]{:S(2)}, u32[]{:S(2)}) async-start(bf16[1,4,32,2,128]{4,2,3,0,1:T(8,128)(2,1)} %fusion.13), calls=%async_computation.1 | async-start | bytes 131072 | tf_op jit(solution)/shard_map/all_to_all | solution.py:30
  55.7 10.6 %all-to-all-start = ((bf16[1,4,32,1024]{3,2,0,1:T(8,128)(2,1)}), bf16[1,4,32,1024]{3,2,0,1:T(8,128)(2,1)S(1)}, u32[]{:S(2)}, u32[]{:S(2)}) async-start(bf16[1,4,32,1024]{3,2,0,1:T(8,128)(2,1)} %bitcast_select_fusion.1), calls=%async_computation | async-start | bytes 524288 | tf_op jit(solution)/shard_map/all_to_all | solution.py:29
  60.5 202.0 %all-reduce.2.cloned.1.call-start = ((), (), s32[]{:S(2)}) async-start(), calls=%async_computation.3 | async-start | bytes 4194304 | tf_op jit(solution)/shard_map/psum | solution.py:92
Sparse Core Ops, SparseCore 0:
  9.8 133.8 all-gather.1
  153.5 109.0 all-reduce.1
where the time goes:
time: 272 us; the launch traced here: 271 us
  waiting for transfers between devices  161 us (59%)
  blocking collectives  36.8 us (14%)
  matrix products  17.4 us (6%)
  loops' own time  16.1 us (6%)
  between operations  13.5 us (5%)
  starting transfers between devices  10.2 us (4%)
  local copies, waits for them, and re-layouts  9.09 us (3%)
  other arithmetic  7.04 us (3%)
    psum x1, waiting for transfers between devices, local(): lax.psum(partial_value.astype(jnp.bfloat16), 'mp').astype(jnp.float32)  109 us
    all_gather x1, waiting for transfers between devices, local(): lax.all_gather(out_weight, ('dp', 'seq'), axis=1, tiled=True)  45.3 us
    all_gather x1, blocking collectives, local(): lax.all_gather(prompt_keys, 'seq', axis=1, tiled=True)  19.6 us
    all_gather x1, blocking collectives, local(): lax.all_gather(prompt_values, 'seq', axis=1, tiled=True)  17.2 us
    another operation x1, loops' own time, local(): per_head = lax.map(head_output, jnp.arange(local_heads, dtype=jnp.int32))  16.1 us
    dot_general x1, matrix products, local(): jnp.dot(attended, lax.all_gather(out_weight, ('dp', 'seq'), axis=1, tiled...  9.59 us
    all_to_all x1, waiting for transfers between devices, local(): lax.all_to_all(sorted_q, 'dp', split_axis=1, concat_axis=1, tiled=True)  5.75 us
  transfers between devices with their start and end apart: 4, of which 3 were waited for; matrix products, arithmetic and copies ran while one was open for 8% of the time, Pallas kernels for 0%

commit v1 on v0

v1 whole, which is shorter than its diff:
```python
import math

import jax
import jax.numpy as jnp
from jax import lax
from jax.experimental import pallas as pl
from jax.experimental.pallas import tpu as pltpu
from jax.sharding import PartitionSpec as P

HD = 128
MESH = pl.DeviceIdType.MESH
Y_OFF = (0, 1, 3, 2)
X_OFF = (2, 1, 3, 0)


class Ids:
    def __init__(self):
        self.n = 0

    def take(self, *dims):
        base = self.n
        size = math.prod(dims)
        self.n += size

        def at(*idx):
            flat = 0
            for d, i in zip(dims, idx):
                flat = flat * d + i
            return base + flat

        return at


IDS = Ids()
S_Q = IDS.take(4)
S_K = IDS.take(4)
S_V = IDS.take(4)
S_KS = IDS.take(4)
S_VS = IDS.take(4)
S_WSIB = IDS.take(1)
S_WSWAP = IDS.take(2)
S_WRING = IDS.take(2, 2, 2)
S_WSHARE = IDS.take(2, 5)
S_A = IDS.take(4, 4, 2)
S_H = IDS.take(2, 4)
S_F = IDS.take(2, 4)
S_G = IDS.take(2, 8)
N_SEM = IDS.n


def kernel(
    prompt_of, lengths, q_ref, kv_ref, k_ref, v_ref, w_ref, out_ref,
    qs, qb, kb, vb, wb, ab, cs, rh, rf, fs, gb, ss, rs, lsem,
):
    y = lax.axis_index("dp")
    seq = lax.axis_index("seq")
    mp = lax.axis_index("mp")
    zh, c = seq // 2, seq % 2
    x, zl = mp // 2, mp % 2
    z = zh * 2 + zl
    half_k = w_ref.shape[0] // 2
    cap = q_ref.shape[1]
    width = q_ref.shape[2]
    heads = width // HD

    def at_y(off):
        return (lax.rem(y + off, 4), seq, mp)

    def at_x(off):
        return (y, seq, lax.rem(x + off, 4) * 2 + zl)

    def at_z(off):
        zz = lax.rem(z + off, 8)
        return (y, (zz // 2) * 2 + c, x * 2 + zz % 2)

    sibling = (y, zh * 2 + 1 - c, mp)

    def copy(src, dst, send, recv, to):
        return pltpu.make_async_remote_copy(
            src_ref=src, dst_ref=dst, send_sem=ss.at[send], recv_sem=rs.at[recv],
            device_id=to, device_id_type=MESH,
        )

    pending = []

    def send(src, dst, sem, to):
        cp = copy(src, dst, sem, sem, to)
        cp.start()
        pending.append(cp)
        return cp

    def arrived(dst, sem):
        copy(dst, dst, sem, sem, sibling).wait_recv()

    barrier = pltpu.get_barrier_semaphore()
    peers = [at_y(1), at_y(2), at_y(3), sibling, at_x(1), at_x(3)]
    peers += [at_z(m) for m in range(1, 8)]
    peers.append((y, zh * 2 + 1 - c, x * 2 + 1 - zl))
    for peer in peers:
        pl.semaphore_signal(barrier, inc=1, device_id=peer, device_id_type=MESH)

    source = y * 8 + seq
    for k in range(4):
        prompt = lax.rem(y + k, 4)
        slot = jnp.int32(0)
        for j in range(1, 4):
            slot = jnp.where(prompt_of[source, j] == prompt, j, slot)
        if k == 0:
            qb[y, :, 0:width] = q_ref[slot]
            qb[y, :, width : width + 2 * HD] = kv_ref[slot]
        else:
            qs[k, :, 0:width] = q_ref[slot]
            qs[k, :, width : width + 2 * HD] = kv_ref[slot]
    rows_of = lambda s: pl.ds(pl.multiple_of(s * HD, HD), HD)
    kb[rows_of(seq), :] = k_ref[0]
    vb[rows_of(seq), :] = v_ref[0]

    pl.semaphore_wait(barrier, len(peers))

    q_sends = [send(qs.at[k], qb.at[y], S_Q(k), at_y(k)) for k in (2, 1, 3)]
    for m in (2, 1, 3):
        send(kb.at[rows_of(seq)], kb.at[rows_of(seq)], S_K(m), at_z(2 * m))
    for m in (2, 1, 3):
        send(vb.at[rows_of(seq)], vb.at[rows_of(seq)], S_V(m), at_z(2 * m))
    send(kb.at[rows_of(seq)], kb.at[rows_of(seq)], S_KS(0), sibling)
    send(vb.at[rows_of(seq)], vb.at[rows_of(seq)], S_VS(0), sibling)

    keeps = zl == c
    w_local = pltpu.make_async_copy(w_ref, wb.at[y, zl], lsem)
    w_sib = copy(w_ref, wb.at[y, zl], S_WSIB(0), S_WSIB(0), sibling)

    @pl.when(keeps)
    def _():
        w_local.start()
        w_sib.start()
        w_local.wait()

    @pl.when(jnp.logical_not(keeps))
    def _():
        w_sib.wait_recv()

    mine = lambda core: pl.ds(pl.multiple_of(core * half_k, half_k), half_k)
    quarter = half_k // 2
    part = lambda core, h: pl.ds(pl.multiple_of(core * half_k + h * quarter, quarter), quarter)

    def w_start(r, kh):
        block = wb.at[y, kh, mine(c)]
        send(block, block, S_WRING(r, 0, 0), at_y(1))
        send(block, block, S_WRING(r, 0, 1), at_y(3))

    def w_share(r, n, slot):
        send(slot, slot, S_WSHARE(r, n), sibling)

    def w_relay(r, kh):
        left, right = lax.rem(y + 3, 4), lax.rem(y + 1, 4)
        arrived(wb.at[left, kh, mine(c)], S_WRING(r, 0, 0))
        slot = wb.at[left, kh, part(c, 0)]
        send(slot, slot, S_WRING(r, 1, 0), at_y(1))
        w_share(r, 1, wb.at[left, kh, mine(c)])
        arrived(wb.at[right, kh, mine(c)], S_WRING(r, 0, 1))
        slot = wb.at[right, kh, part(c, 1)]
        send(slot, slot, S_WRING(r, 1, 1), at_y(3))
        w_share(r, 2, wb.at[right, kh, mine(c)])

    def w_finish(r, kh):
        far = lax.rem(y + 2, 4)
        for h in range(2):
            slot = wb.at[far, kh, part(c, h)]
            arrived(slot, S_WRING(r, 1, h))
            w_share(r, 3 + h, slot)

    def w_shared(r, n):
        kh = zl if r == 0 else 1 - zl
        other = 1 - c
        if n == 0:
            slot = wb.at[y, kh, mine(other)]
        elif n == 1:
            slot = wb.at[lax.rem(y + 3, 4), kh, mine(other)]
        elif n == 2:
            slot = wb.at[lax.rem(y + 1, 4), kh, mine(other)]
        else:
            slot = wb.at[lax.rem(y + 2, 4), kh, part(other, n - 3)]
        arrived(slot, S_WSHARE(r, n))

    for cp in q_sends:
        cp.wait_send()
        pending.remove(cp)
    w_start(0, zl)

    for m in (1, 3, 2):
        block = rows_of(lax.rem(zh + 4 - m, 4) * 2 + c)
        arrived(kb.at[block], S_K(m))
        send(kb.at[block], kb.at[block], S_KS(m), sibling)
    for m in (1, 3, 2):
        block = rows_of(lax.rem(zh + 4 - m, 4) * 2 + c)
        arrived(vb.at[block], S_V(m))
        send(vb.at[block], vb.at[block], S_VS(m), sibling)

    swaps = []
    for j in range(2):
        rows = pl.ds(j * half_k, half_k)
        swaps.append(
            copy(
                w_ref.at[rows], wb.at[y, zl, rows], S_WSWAP(j), S_WSWAP(0),
                (y, zh * 2 + j, x * 2 + 1 - zl),
            )
        )

    @pl.when(jnp.logical_not(keeps))
    def _():
        for cp in swaps:
            cp.start()

    for m in range(4):
        block = rows_of(lax.rem(zh + 4 - m, 4) * 2 + 1 - c)
        arrived(kb.at[block], S_KS(m))
        arrived(vb.at[block], S_VS(m))

    factor = math.log2(math.e) / math.sqrt(HD)

    def a_slot(i, off, rows=None):
        zz = lax.rem(z + off + 8, 8)
        base = pl.multiple_of((zz // 2) * cap, cap)
        if rows is None:
            return ab.at[i, zz % 2, pl.ds(base, cap)]
        return ab.at[i, zz % 2, pl.ds(pl.multiple_of(base + rows * (cap // 2), cap // 2), cap // 2)]

    def attend(i):
        d = lax.rem(x + X_OFF[i], 4)
        if True:
            for k in (1, 2, 3):
                @pl.when(d == lax.rem(y + 4 - k, 4))
                def _():
                    arrived(qb.at[lax.rem(y + 4 - k, 4)], S_Q(k))
        src = d * 8 + seq
        length = jnp.int32(0)
        for j in range(4):
            length = length + jnp.where(prompt_of[src, j] == y, lengths[src, j], 0)
        q = jnp.concatenate([qb[d, :, h * HD : (h + 1) * HD] for h in range(heads)], axis=0)
        near_k = qb[d, :, width : width + HD]
        near_v = qb[d, :, width + HD : width + 2 * HD]
        nt = (((1,), (1,)), ((), ()))
        far = lax.dot_general(q, kb[...], nt, preferred_element_type=jnp.float32)
        near = lax.dot_general(q, near_k, nt, preferred_element_type=jnp.float32)
        token = lax.rem(lax.broadcasted_iota(jnp.int32, near.shape, 0), cap)
        key = lax.broadcasted_iota(jnp.int32, near.shape, 1)
        near = jnp.where(token >= key, near, -jnp.inf)
        top = jnp.maximum(
            jnp.max(far, axis=1, keepdims=True), jnp.max(near, axis=1, keepdims=True)
        )
        far = jnp.exp2((far - top) * factor)
        near = jnp.exp2((near - top) * factor)
        total = jnp.sum(far, axis=1, keepdims=True) + jnp.sum(near, axis=1, keepdims=True)
        result = jnp.dot(far.astype(jnp.bfloat16), vb[...], preferred_element_type=jnp.float32)
        result = result + jnp.dot(
            near.astype(jnp.bfloat16), near_v, preferred_element_type=jnp.float32
        )
        row = lax.rem(lax.broadcasted_iota(jnp.int32, result.shape, 0), cap)
        result = jnp.where(row < length, result / total, 0.0).astype(jnp.bfloat16)
        base = pl.multiple_of(zh * cap, cap)
        for h in range(heads):
            ab[i, zl, pl.ds(base, cap), h * HD : (h + 1) * HD] = result[h * cap : (h + 1) * cap]
        slot = a_slot(i, 0)
        send(slot, slot, S_A(i, 0, 0), at_z(1))
        send(slot, slot, S_A(i, 0, 1), at_z(7))

    def a_relay(i, s):
        slot = a_slot(i, -s)
        arrived(slot, S_A(i, s - 1, 0))
        if s == 3:
            slot = a_slot(i, -s, 0)
        send(slot, slot, S_A(i, s, 0), at_z(1))
        slot = a_slot(i, s)
        arrived(slot, S_A(i, s - 1, 1))
        if s == 3:
            slot = a_slot(i, s, 1)
        send(slot, slot, S_A(i, s, 1), at_z(7))

    def product(i, k):
        yk = lax.rem(y + Y_OFF[k], 4)
        return jnp.dot(ab[i, 0], wb[yk, 0], preferred_element_type=jnp.float32) + jnp.dot(
            ab[i, 1], wb[yk, 1], preferred_element_type=jnp.float32
        )

    def w_needed(k):
        if k == 0:
            w_shared(1, 0)
        elif k == 1:
            w_shared(0, 2)
            w_shared(1, 2)
        elif k == 2:
            w_shared(0, 1)
            w_shared(1, 1)
        else:
            w_finish(1, 1 - zl)
            for r in range(2):
                w_shared(r, 3)
                w_shared(r, 4)

    rows = cs.shape[2]
    half = rows // 2

    def project(i):
        a_far = [a_slot(i, 4, h) for h in range(2)]
        arrived(a_far[0], S_A(i, 3, 0))
        arrived(a_far[1], S_A(i, 3, 1))
        for k in range(4):
            if i == 0:
                w_needed(k)
            value = product(i, k)
            if i == 0:
                cs[0, k] = value.astype(jnp.bfloat16)
                send(cs.at[0, k, 0:half], rh.at[0, k], S_H(0, k), at_x(1))
                send(cs.at[0, k, half:rows], rh.at[1, k], S_H(1, k), at_x(3))
            elif i == 1:
                arrived(rh.at[0, k], S_H(0, k))
                top = value[0:half] + rh[0, k].astype(jnp.float32)
                cs[1, k, 0:half] = top.astype(jnp.bfloat16)
                cs[1, k, half:rows] = value[half:rows].astype(jnp.bfloat16)
                send(cs.at[1, k], rf.at[0, k], S_F(0, k), at_x(1))
            elif i == 2:
                arrived(rh.at[1, k], S_H(1, k))
                low = value[half:rows] + rh[1, k].astype(jnp.float32)
                cs[2, k, 0:half] = value[0:half].astype(jnp.bfloat16)
                cs[2, k, half:rows] = low.astype(jnp.bfloat16)
                send(cs.at[2, k], rf.at[1, k], S_F(1, k), at_x(3))
            else:
                arrived(rf.at[0, k], S_F(0, k))
                arrived(rf.at[1, k], S_F(1, k))
                value = value + rf[0, k].astype(jnp.float32) + rf[1, k].astype(jnp.float32)
                fs[k] = value.astype(jnp.bfloat16)
                if k % 2 == 1:
                    g = k // 2
                    for m in range(1, 8):
                        zz = lax.rem(z + m, 8)
                        block = pl.ds(pl.multiple_of(zz * 16, 16), 16)
                        send(
                            fs.at[2 * g : 2 * g + 2, block], gb.at[2 * g : 2 * g + 2, z],
                            S_G(g, m), at_z(m),
                        )

    for t in range(8):
        if t < 4:
            attend(t)
        for s in (3, 2, 1):
            if 0 <= t - s < 4:
                a_relay(t - s, s)
        if t == 1:
            arrived(wb.at[y, 1 - zl, mine(c)], S_WSWAP(0))
            w_start(1, 1 - zl)
            w_share(1, 0, wb.at[y, 1 - zl, mine(c)])
            w_relay(0, zl)
        if t == 3:
            w_finish(0, zl)
            w_relay(1, 1 - zl)
        if t >= 4:
            project(t - 4)

    for g in range(2):
        for k in (2 * g, 2 * g + 1):
            yk = lax.rem(y + Y_OFF[k], 4)
            own = pl.ds(pl.multiple_of(z * 16, 16), 16)
            gb[k, z] = fs[k, own]
        for m in range(1, 8):
            zz = lax.rem(z + 8 - m, 8)
            arrived(gb.at[2 * g : 2 * g + 2, zz], S_G(g, m))
        for k in (2 * g, 2 * g + 1):
            yk = lax.rem(y + Y_OFF[k], 4)
            for zz in range(8):
                columns = pl.ds(pl.multiple_of((yk * 8 + zz) * 256, 256), 256)
                out_ref[:, columns] = gb[k, zz]

    for cp in pending:
        cp.wait_send()

    @pl.when(keeps)
    def _():
        w_sib.wait_send()

    @pl.when(jnp.logical_not(keeps))
    def _():
        for cp in swaps:
            cp.wait_send()


def local(queries, resp_kv, prompt_keys, prompt_values, out_weight, lengths, prompt_of):
    slots, cap, width = queries.shape[1:]
    tokens = prompt_keys.shape[1]
    k_rows, columns = out_weight.shape
    q = queries.reshape(slots, cap, width)
    kv = resp_kv.reshape(slots, cap, 2 * HD)
    packed = width + 2 * HD
    bf = jnp.bfloat16
    vmem = pl.BlockSpec(memory_space=pltpu.VMEM)
    smem = pl.BlockSpec(memory_space=pltpu.SMEM)
    return pl.pallas_call(
        kernel,
        out_shape=jax.ShapeDtypeStruct((16, 32 * columns), bf),
        in_specs=[smem, smem, vmem, vmem, vmem, vmem, pl.BlockSpec(memory_space=pl.ANY)],
        out_specs=vmem,
        scratch_shapes=[
            pltpu.VMEM((4, cap, packed), bf),
            pltpu.VMEM((4, cap, packed), bf),
            pltpu.VMEM((8 * tokens, HD), bf),
            pltpu.VMEM((8 * tokens, HD), bf),
            pltpu.VMEM((4, 2, k_rows, columns), bf),
            pltpu.VMEM((4, 2, 4 * cap, width), bf),
            pltpu.VMEM((3, 4, 4 * cap, columns), bf),
            pltpu.VMEM((2, 4, 2 * cap, columns), bf),
            pltpu.VMEM((2, 4, 4 * cap, columns), bf),
            pltpu.VMEM((4, 4 * cap, columns), bf),
            pltpu.VMEM((4, 8, 16, columns), bf),
            pltpu.SemaphoreType.DMA((N_SEM,)),
            pltpu.SemaphoreType.DMA((N_SEM,)),
            pltpu.SemaphoreType.DMA,
        ],
        compiler_params=pltpu.CompilerParams(
            collective_id=0, has_side_effects=True, vmem_limit_bytes=48 * 2**20
        ),
        cost_estimate=pl.CostEstimate(
            flops=2_700_000_000, bytes_accessed=2_000_000, transcendentals=1_100_000
        ),
        name="attend_project",
    )(prompt_of, lengths, q, kv, prompt_keys, prompt_values, out_weight)


def solution(mesh):
    placed = (
        P(("dp", "seq"), None, None, "mp"),
        P(("dp", "seq"), None, None, None, "mp"),
        P("dp", "seq", "mp"),
        P("dp", "seq", "mp"),
        P("mp", ("dp", "seq")),
        P(),
        P(),
    )
    return jax.shard_map(
        local, mesh=mesh, in_specs=placed, out_specs=P(("dp", "seq", "mp"), None), check_vma=False
    )
```

time: 272 us -> 69 us (0.25)
  waiting for transfers between devices: 161 us -> 0 us
  Pallas kernels: 0 us -> 64 us
  blocking collectives: 36.8 us -> 0 us
  matrix products: 17.4 us -> 0 us
  loops' own time: 16.1 us -> 0 us
  between operations: 13.5 us -> 0.04 us
  starting transfers between devices: 10.2 us -> 0 us
  other arithmetic: 7.04 us -> 0 us
  local copies, waits for them, and re-layouts: 9.09 us -> 4.46 us
    psum x1 -> x0, waiting for transfers between devices: 109 us -> none  [local(): lax.psum(partial_value.astype(jnp.bfloat16), 'mp').astype(jnp.float32)]
    pallas_call x0 -> x1, Pallas kernels: none -> 64 us  [local(): pl.pallas_call(kernel, out_shape=jax.ShapeDtypeStruct((16, 32 * columns),...]
    all_gather x1 -> x0, waiting for transfers between devices: 45.3 us -> none  [local(): lax.all_gather(out_weight, ('dp', 'seq'), axis=1, tiled=True)]
    all_gather x2 -> x0, blocking collectives: 36.8 us -> none  [the longest x1 19.6 us: local(): lax.all_gather(prompt_keys, 'seq', axis=1, tiled=True)]
    dot_general x33 -> x0, matrix products: 17.4 us -> none  [the longest x1 9.59 us: local(): jnp.dot(attended, lax.all_gather(out_weight, ('dp', 'seq'), axis=1, tiled...]
    another operation x1 -> x0, loops' own time: 16.1 us -> none  [local(): per_head = lax.map(head_output, jnp.arange(local_heads, dtype=jnp.int32))]
    all_to_all x2 -> x0, starting transfers between devices: 10.2 us -> none  [the longest x1 5.43 us: local(): lax.all_to_all(sorted_kv, 'dp', split_axis=1, concat_axis=1, tiled=True)]
    dynamic_slice x18 -> x0, local copies, waits for them, and re-layouts: 5.84 us -> none  [the longest x8 4.69 us: local(): per_head = lax.map(head_output, jnp.arange(local_heads, dtype=jnp.int32))]
  transfers between devices with their start and end apart: 4 -> 0, of which waited for: 3 -> 0; matrix products, arithmetic and copies ran while one was open for 8% -> 0% of each run, Pallas kernels for 0% -> 0%
where the time goes in v1:
time: 69 us; the launch traced here: 68.5 us
  Pallas kernels  64 us (93%)
  local copies, waits for them, and re-layouts  4.46 us (6%)
    pallas_call x1, Pallas kernels, local(): pl.pallas_call(kernel, out_shape=jax.ShapeDtypeStruct((16, 32 * columns),...  64 us
    unnamed x13, local copies, waits for them, and re-layouts  3.56 us

profile of v1, /device:TPU:8, one launch (start us, length us, event | category | flops | bytes accessed | tf_op | source)
XLA Modules:
  0.0 68.5 jit_solution(9848713528593499665)
XLA Ops:
  0.0 0.0 copy-start.4
  0.0 0.8 %copy.9.lengths = s32[32,4]{1,0:T(8,128)S(1)} copy(s32[32,4]{0,1:T(4,128)} %param.12) | data formatting | bytes 1024 | tf_op args[5]
  0.8 0.0 copy-done.4
  0.8 0.1 copy.8.prompt_of
  0.9 0.0 copy-start.2
  0.9 0.0 copy-start.3
  0.9 0.9 %reshape.7.kv_ref = bf16[4,32,256]{2,1,0:T(8,128)(2,1)S(1)} reshape(bf16[1,4,32,2,128]{4,3,2,1,0:T(2,128)(2,1)} %param.8) | data formatting | bytes 131072 | tf_op jit(solution)/shard_map/reshape | solution.py:391
  1.8 0.0 copy-done.2
  1.8 0.0 copy-done.3
  1.8 0.0 copy-start
  1.8 1.0 %copy-done = bf16[1024,256]{1,0:T(8,128)(2,1)S(1)} copy-done((bf16[1024,256]{1,0:T(8,128)(2,1)S(1)}, bf16[1024,256]{1,0:T(8,128)(2,1)}, u32[]{:S(2)}) %copy-start) | copy-done | bytes 524312
  2.8 0.0 copy-start.1
  2.8 0.9 %copy-done.1 = bf16[1,4,32,1024]{3,2,1,0:T(8,128)(2,1)S(1)} copy-done((bf16[1,4,32,1024]{3,2,1,0:T(8,128)(2,1)S(1)}, bf16[1,4,32,1024]{3,2,1,0:T(8,128)(2,1)}, u32[]{:S(2)}) %copy-start.1) | copy-done | bytes 262168
  3.8 64.0 %attend_project.1 = bf16[16,8192]{1,0:T(8,128)(2,1)S(1)} custom-call(s32[32,4]{1,0:T(8,128)S(1)} %copy.8.prompt_of, s32[32,4]{1,0:T(8,128)S(1)} %copy.9.lengths, bf16[4,32,1024]{2,1,0:T(8,128)(2,1)S(1)} %bitcast.1, bf16[4,32,256]{2,1,0:T(8,128)(2,1)S(1)} %reshape.7.kv_ref, bf16[1,128,128]{2,1,0:T(8,128)(2,1)S(1)} %copy-done.2, ...), custom_call_target="tpu_custom_call" | custom-call | flops 2700000000 | bytes 2000000 | tf_op jit(solution)/shard_map/attend_project/pallas_call | solution.py:396
  67.8 0.7 %copy.11 = bf16[16,8192]{1,0:T(8,128)(2,1)} copy(bf16[16,8192]{1,0:T(8,128)(2,1)S(1)} %attend_project.1) | data formatting | bytes 524288
Async XLA Ops:
  0.0 0.8 %copy-start.4 = (s32[32,4]{0,1:T(4,128)S(1)}, s32[32,4]{0,1:T(4,128)}, u32[]{:S(2)}) copy-start(s32[32,4]{0,1:T(4,128)} %param.13) | copy-start | bytes 1540
  0.9 0.9 %copy-start.2 = (bf16[1,128,128]{2,1,0:T(8,128)(2,1)S(1)}, bf16[1,128,128]{2,1,0:T(8,128)(2,1)}, u32[]{:S(2)}) copy-start(bf16[1,128,128]{2,1,0:T(8,128)(2,1)} %k_ref.1) | copy-start | bytes 98308
  0.9 0.9 %copy-start.3 = (bf16[1,128,128]{2,1,0:T(8,128)(2,1)S(1)}, bf16[1,128,128]{2,1,0:T(8,128)(2,1)}, u32[]{:S(2)}) copy-start(bf16[1,128,128]{2,1,0:T(8,128)(2,1)} %v_ref.1) | copy-start | bytes 98308
  1.8 1.0 %copy-start = (bf16[1024,256]{1,0:T(8,128)(2,1)S(1)}, bf16[1024,256]{1,0:T(8,128)(2,1)}, u32[]{:S(2)}) copy-start(bf16[1024,256]{1,0:T(8,128)(2,1)} %w_ref.1) | copy-start | bytes 1572868
  2.8 0.9 %copy-start.1 = (bf16[1,4,32,1024]{3,2,1,0:T(8,128)(2,1)S(1)}, bf16[1,4,32,1024]{3,2,1,0:T(8,128)(2,1)}, u32[]{:S(2)}) copy-start(bf16[1,4,32,1024]{3,2,1,0:T(8,128)(2,1)} %param.7) | copy-start | bytes 786436

commit v2 on v1

v2 whole, which is shorter than its diff:
```python
import math

import jax
import jax.numpy as jnp
from jax import lax
from jax.experimental import pallas as pl
from jax.experimental.pallas import tpu as pltpu
from jax.sharding import PartitionSpec as P

HD = 128
MESH = pl.DeviceIdType.MESH
Y_OFF = (0, 1, 3, 2)
BATCHES = ((0, 1), (2, 3))
GROUPS = ((0, 3), (3, 4))


class Ids:
    def __init__(self):
        self.n = 0

    def take(self, *dims):
        base = self.n
        size = math.prod(dims)
        self.n += size

        def at(*idx):
            flat = 0
            for d, i in zip(dims, idx):
                flat = flat * d + i
            return base + flat

        return at


IDS = Ids()
S_Q = IDS.take(4)
S_K = IDS.take(4)
S_V = IDS.take(4)
S_KS = IDS.take(4)
S_VS = IDS.take(4)
S_WSIB = IDS.take(1)
S_WSWAP = IDS.take(2)
S_WRING = IDS.take(2, 2, 2)
S_WSHARE = IDS.take(2, 5)
S_A = IDS.take(len(BATCHES), 4, 2)
S_R = IDS.take(4, len(GROUPS), 4)
S_G = IDS.take(len(GROUPS), 8)
N_SEM = IDS.n


def kernel(
    prompt_hbm, length_hbm, q_hbm, kv_hbm, k_hbm, v_hbm, w_ref, out_ref,
    prompt_of, lengths, q_ref, kv_ref,
    qs, qb, kb, vb, wb, ab, cs, rb, fs, gb, ss, rs, lsem,
):
    y = lax.axis_index("dp")
    seq = lax.axis_index("seq")
    mp = lax.axis_index("mp")
    zh, c = seq // 2, seq % 2
    x, zl = mp // 2, mp % 2
    z = zh * 2 + zl
    half_k = w_ref.shape[0] // 2
    columns = w_ref.shape[1]
    cap = q_ref.shape[1]
    width = q_ref.shape[2]
    heads = width // HD
    half_cap = cap // 2

    def at_y(off):
        return (lax.rem(y + off, 4), seq, mp)

    def at_x(off):
        return (y, seq, lax.rem(x + off, 4) * 2 + zl)

    def at_z(off):
        zz = lax.rem(z + off, 8)
        return (y, (zz // 2) * 2 + c, x * 2 + zz % 2)

    sibling = (y, zh * 2 + 1 - c, mp)

    def copy(src, dst, send, recv, to):
        return pltpu.make_async_remote_copy(
            src_ref=src, dst_ref=dst, send_sem=ss.at[send], recv_sem=rs.at[recv],
            device_id=to, device_id_type=MESH,
        )

    pending = []

    def send(src, dst, sem, to):
        cp = copy(src, dst, sem, sem, to)
        cp.start()
        pending.append(cp)
        return cp

    def arrived(dst, sem):
        copy(dst, dst, sem, sem, sibling).wait_recv()

    rows_of = lambda s: pl.ds(pl.multiple_of(s * HD, HD), HD)
    own_rows = rows_of(seq)
    fetches = [
        pltpu.make_async_copy(src, dst, lsem.at[n])
        for n, (src, dst) in enumerate(
            (
                (prompt_hbm, prompt_of),
                (length_hbm, lengths),
                (q_hbm.at[0], q_ref),
                (kv_hbm.at[0], kv_ref),
                (k_hbm.at[0], kb.at[own_rows]),
                (v_hbm.at[0], vb.at[own_rows]),
            )
        )
    ]
    for cp in fetches:
        cp.start()
    keeps = zl == c
    w_local = pltpu.make_async_copy(w_ref, wb.at[y, zl], lsem.at[len(fetches)])

    @pl.when(keeps)
    def _():
        w_local.start()

    barrier = pltpu.get_barrier_semaphore()
    peers = [at_y(1), at_y(2), at_y(3), sibling, at_x(1), at_x(2), at_x(3)]
    peers += [at_z(m) for m in range(1, 8)]
    peers.append((y, zh * 2 + 1 - c, x * 2 + 1 - zl))
    for peer in peers:
        pl.semaphore_signal(barrier, inc=1, device_id=peer, device_id_type=MESH)

    for cp in fetches:
        cp.wait()
    source = y * 8 + seq
    for k in range(4):
        prompt = lax.rem(y + k, 4)
        slot = jnp.int32(0)
        for j in range(1, 4):
            slot = jnp.where(prompt_of[j, source] == prompt, j, slot)
        to, at = (qb, y) if k == 0 else (qs, k)
        to[at, :, 0:width] = q_ref[slot]
        pair = kv_ref[slot]
        to[at, :, width : width + HD] = pair[:, 0, :]
        to[at, :, width + HD : width + 2 * HD] = pair[:, 1, :]

    pl.semaphore_wait(barrier, len(peers))

    for m in (2, 1, 3):
        send(kb.at[own_rows], kb.at[own_rows], S_K(m), at_z(2 * m))
    for k in (2, 1, 3):
        send(qs.at[k], qb.at[y], S_Q(k), at_y(k))
    for m in (2, 1, 3):
        send(vb.at[own_rows], vb.at[own_rows], S_V(m), at_z(2 * m))
    send(kb.at[own_rows], kb.at[own_rows], S_KS(0), sibling)
    send(vb.at[own_rows], vb.at[own_rows], S_VS(0), sibling)

    w_sib = copy(w_ref, wb.at[y, zl], S_WSIB(0), S_WSIB(0), sibling)

    @pl.when(keeps)
    def _():
        w_sib.start()
        w_local.wait()

    @pl.when(jnp.logical_not(keeps))
    def _():
        w_sib.wait_recv()

    mine = lambda core: pl.ds(pl.multiple_of(core * half_k, half_k), half_k)
    quarter = half_k // 2
    part = lambda core, h: pl.ds(pl.multiple_of(core * half_k + h * quarter, quarter), quarter)
    late = 1 - zl

    def w_start(r, kh):
        block = wb.at[y, kh, mine(c)]
        send(block, block, S_WRING(r, 0, 0), at_y(1))
        send(block, block, S_WRING(r, 0, 1), at_y(3))

    def w_share(r, n, slot):
        send(slot, slot, S_WSHARE(r, n), sibling)

    def w_relay(r, kh):
        left, right = lax.rem(y + 3, 4), lax.rem(y + 1, 4)
        arrived(wb.at[left, kh, mine(c)], S_WRING(r, 0, 0))
        slot = wb.at[left, kh, part(c, 0)]
        send(slot, slot, S_WRING(r, 1, 0), at_y(1))
        w_share(r, 1, wb.at[left, kh, mine(c)])
        arrived(wb.at[right, kh, mine(c)], S_WRING(r, 0, 1))
        slot = wb.at[right, kh, part(c, 1)]
        send(slot, slot, S_WRING(r, 1, 1), at_y(3))
        w_share(r, 2, wb.at[right, kh, mine(c)])

    def w_finish(r, kh):
        far = lax.rem(y + 2, 4)
        for h in range(2):
            slot = wb.at[far, kh, part(c, h)]
            arrived(slot, S_WRING(r, 1, h))
            w_share(r, 3 + h, slot)

    def w_shared(r, n):
        kh = zl if r == 0 else 1 - zl
        other = 1 - c
        if n == 0:
            slot = wb.at[y, kh, mine(other)]
        elif n == 1:
            slot = wb.at[lax.rem(y + 3, 4), kh, mine(other)]
        elif n == 2:
            slot = wb.at[lax.rem(y + 1, 4), kh, mine(other)]
        else:
            slot = wb.at[lax.rem(y + 2, 4), kh, part(other, n - 3)]
        arrived(slot, S_WSHARE(r, n))

    def w_near():
        w_shared(1, 0)
        for r in range(2):
            w_shared(r, 1)
            w_shared(r, 2)

    def w_far():
        for r in range(2):
            w_shared(r, 3)
            w_shared(r, 4)

    def forward(ref, first, then):
        for m in (1, 3, 2):
            block = rows_of(lax.rem(zh + 4 - m, 4) * 2 + c)
            arrived(ref.at[block], first(m))
            send(ref.at[block], ref.at[block], then(m), sibling)

    def shared(ref, then):
        for m in range(4):
            block = rows_of(lax.rem(zh + 4 - m, 4) * 2 + 1 - c)
            arrived(ref.at[block], then(m))

    swaps = []
    for j in range(2):
        rows = pl.ds(j * half_k, half_k)
        swaps.append(
            copy(
                w_ref.at[rows], wb.at[y, zl, rows], S_WSWAP(j), S_WSWAP(0),
                (y, zh * 2 + j, x * 2 + 1 - zl),
            )
        )

    def swap_start():
        @pl.when(jnp.logical_not(keeps))
        def _():
            for cp in swaps:
                cp.start()

    def swap_end():
        arrived(wb.at[y, late, mine(c)], S_WSWAP(0))
        w_start(1, late)
        w_share(1, 0, wb.at[y, late, mine(c)])

    factor = math.log2(math.e) / math.sqrt(HD)

    def attend(i):
        d = lax.rem(y + Y_OFF[i], 4)
        if i:
            arrived(qb.at[d], S_Q((4 - Y_OFF[i]) % 4))
        src = d * 8 + seq
        length = jnp.int32(0)
        for j in range(4):
            length = length + jnp.where(prompt_of[j, src] == y, lengths[j, src], 0)
        q = jnp.concatenate([qb[d, :, h * HD : (h + 1) * HD] for h in range(heads)], axis=0)
        near_k = qb[d, :, width : width + HD]
        near_v = qb[d, :, width + HD : width + 2 * HD]
        nt = (((1,), (1,)), ((), ()))
        far = lax.dot_general(q, kb[...], nt, preferred_element_type=jnp.float32)
        near = lax.dot_general(q, near_k, nt, preferred_element_type=jnp.float32)
        token = lax.rem(lax.broadcasted_iota(jnp.int32, near.shape, 0), cap)
        key = lax.broadcasted_iota(jnp.int32, near.shape, 1)
        near = jnp.where(token >= key, near, -jnp.inf)
        top = jnp.maximum(
            jnp.max(far, axis=1, keepdims=True), jnp.max(near, axis=1, keepdims=True)
        )
        far = jnp.exp2((far - top) * factor)
        near = jnp.exp2((near - top) * factor)
        total = jnp.sum(far, axis=1, keepdims=True) + jnp.sum(near, axis=1, keepdims=True)
        result = jnp.dot(far.astype(jnp.bfloat16), vb[...], preferred_element_type=jnp.float32)
        result = result + jnp.dot(
            near.astype(jnp.bfloat16), near_v, preferred_element_type=jnp.float32
        )
        row = lax.rem(lax.broadcasted_iota(jnp.int32, result.shape, 0), cap)
        result = jnp.where(row < length, result / total, 0.0).astype(jnp.bfloat16)
        for h in range(heads):
            ab[zh, zl, i * cap : (i + 1) * cap, h * HD : (h + 1) * HD] = (
                result[h * cap : (h + 1) * cap]
            )

    def a_slot(b, off, h=None):
        zz = lax.rem(z + off + 8, 8)
        first, size = BATCHES[b][0] * cap, len(BATCHES[b]) * cap
        if h is not None:
            size = size // 2
            first = first + h * size
        return ab.at[zz // 2, zz % 2, first : first + size]

    def a_start(b):
        for i in BATCHES[b]:
            attend(i)
        slot = a_slot(b, 0)
        send(slot, slot, S_A(b, 0, 0), at_z(1))
        send(slot, slot, S_A(b, 0, 1), at_z(7))

    def a_relay(b, s):
        slot = a_slot(b, -s)
        arrived(slot, S_A(b, s - 1, 0))
        if s == 3:
            slot = a_slot(b, -s, 0)
        send(slot, slot, S_A(b, s, 0), at_z(1))
        slot = a_slot(b, s)
        arrived(slot, S_A(b, s - 1, 1))
        if s == 3:
            slot = a_slot(b, s, 1)
        send(slot, slot, S_A(b, s, 1), at_z(7))

    def a_last(b):
        for h in range(2):
            arrived(a_slot(b, 4, h), S_A(b, 3, h))

    def pair(p):
        off = (0, 3 - 2 * zl, 1 + 2 * zl, 2)[p]
        return lax.rem(zh + off, 4)

    def cols(g):
        first, last = GROUPS[g]
        return slice(first * columns, last * columns)

    def chunk_of(xx):
        u = lax.rem(xx - y + 4, 4)
        return u + u // 2 - 2 * (u // 2) * (u % 2)

    def block_of(xx):
        return pl.ds(pl.multiple_of(chunk_of(xx) * cap, cap), cap)

    def project(p, g):
        zz = pair(p)
        for k in range(*GROUPS[g]):
            yk = lax.rem(y + Y_OFF[k], 4)
            value = jnp.dot(ab[zz, 0], wb[yk, 0], preferred_element_type=jnp.float32)
            value = value + jnp.dot(ab[zz, 1], wb[yk, 1], preferred_element_type=jnp.float32)
            cs[p, :, k * columns : (k + 1) * columns] = value.astype(jnp.bfloat16)
        for off in (2, 1, 3):
            rows = block_of(lax.rem(x + off, 4))
            send(
                cs.at[p, rows, cols(g)], rb.at[p, off, :, cols(g)], S_R(p, g, off), at_x(off)
            )

    def reduce(p, g):
        value = cs[p, block_of(x), cols(g)].astype(jnp.float32)
        for off in (1, 3, 2):
            arrived(rb.at[p, off, :, cols(g)], S_R(p, g, off))
            value = value + rb[p, off, :, cols(g)].astype(jnp.float32)
        fs[p, :, cols(g)] = value.astype(jnp.bfloat16)
        zz = pair(p)
        for t in range(2):
            half = slice(t * half_cap, (t + 1) * half_cap)
            if p == 0:
                @pl.when(zl == t)
                def _():
                    gb[z, :, cols(g)] = fs[p, half, cols(g)]
        if p == 0:
            half = pl.ds(pl.multiple_of(late * half_cap, half_cap), half_cap)
            off = 1 + 6 * zl
            send(
                fs.at[p, half, cols(g)], gb.at[z, :, cols(g)], S_G(g, 0) + off,
                (y, zz * 2 + c, x * 2 + late),
            )
        else:
            for t in range(2):
                half = slice(t * half_cap, (t + 1) * half_cap)
                off = lax.rem(zz * 2 + t - z + 8, 8)
                send(
                    fs.at[p, half, cols(g)], gb.at[z, :, cols(g)], S_G(g, 0) + off,
                    (y, zz * 2 + c, x * 2 + t),
                )

    def collect(g):
        for m in range(8):
            zz = lax.rem(z + 8 - m, 8)
            if m:
                arrived(gb.at[zz, :, cols(g)], S_G(g, 0) + m)
        for k in range(*GROUPS[g]):
            yk = lax.rem(y + Y_OFF[k], 4)
            for zz in range(8):
                place = pl.ds(pl.multiple_of((yk * 8 + zz) * columns, columns), columns)
                out_ref[:, place] = gb[zz, :, k * columns : (k + 1) * columns]

    batches = range(len(BATCHES))
    w_start(0, zl)
    swap_start()
    forward(kb, S_K, S_KS)
    forward(vb, S_V, S_VS)
    shared(kb, S_KS)
    shared(vb, S_VS)
    for b in batches:
        a_start(b)
    swap_end()
    for b in batches:
        a_relay(b, 1)
    w_relay(0, zl)
    for b in batches:
        a_relay(b, 2)
    w_relay(1, late)
    w_near()
    project(0, 0)
    project(1, 0)
    for b in batches:
        a_relay(b, 3)
    reduce(0, 0)
    reduce(1, 0)
    project(2, 0)
    w_finish(0, zl)
    w_finish(1, late)
    w_far()
    project(0, 1)
    project(1, 1)
    project(2, 1)
    reduce(2, 0)
    for b in batches:
        a_last(b)
    project(3, 0)
    project(3, 1)
    reduce(0, 1)
    reduce(1, 1)
    reduce(2, 1)
    reduce(3, 0)
    reduce(3, 1)
    collect(0)
    collect(1)

    for cp in pending:
        cp.wait_send()

    @pl.when(keeps)
    def _():
        w_sib.wait_send()

    @pl.when(jnp.logical_not(keeps))
    def _():
        for cp in swaps:
            cp.wait_send()


def local(queries, resp_kv, prompt_keys, prompt_values, out_weight, lengths, prompt_of):
    slots, cap, width = queries.shape[1:]
    tokens = prompt_keys.shape[1]
    k_rows, columns = out_weight.shape
    packed = width + 2 * HD
    bf = jnp.bfloat16
    hbm = pl.BlockSpec(memory_space=pltpu.HBM)
    return pl.pallas_call(
        kernel,
        out_shape=jax.ShapeDtypeStruct((16, 32 * columns), bf),
        in_specs=[hbm] * 7,
        out_specs=pl.BlockSpec(memory_space=pltpu.VMEM),
        scratch_shapes=[
            pltpu.SMEM(prompt_of.shape[::-1], jnp.int32),
            pltpu.SMEM(lengths.shape[::-1], jnp.int32),
            pltpu.VMEM((slots, cap, width), bf),
            pltpu.VMEM((slots, cap, 2, HD), bf),
            pltpu.VMEM((4, cap, packed), bf),
            pltpu.VMEM((4, cap, packed), bf),
            pltpu.VMEM((8 * tokens, HD), bf),
            pltpu.VMEM((8 * tokens, HD), bf),
            pltpu.VMEM((4, 2, k_rows, columns), bf),
            pltpu.VMEM((4, 2, 4 * cap, width), bf),
            pltpu.VMEM((4, 4 * cap, 4 * columns), bf),
            pltpu.VMEM((4, 4, cap, 4 * columns), bf),
            pltpu.VMEM((4, cap, 4 * columns), bf),
            pltpu.VMEM((8, cap // 2, 4 * columns), bf),
            pltpu.SemaphoreType.DMA((N_SEM,)),
            pltpu.SemaphoreType.DMA((N_SEM,)),
            pltpu.SemaphoreType.DMA((8,)),
        ],
        compiler_params=pltpu.CompilerParams(
            collective_id=0, has_side_effects=True, vmem_limit_bytes=48 * 2**20
        ),
        cost_estimate=pl.CostEstimate(
            flops=2_700_000_000, bytes_accessed=2_000_000, transcendentals=1_100_000
        ),
        name="attend_project",
    )(*[
        pltpu.with_memory_space_constraint(a, pltpu.HBM)
        for a in (
            prompt_of.T, lengths.T, queries, resp_kv, prompt_keys, prompt_values, out_weight
        )
    ])


def solution(mesh):
    placed = (
        P(("dp", "seq"), None, None, "mp"),
        P(("dp", "seq"), None, None, None, "mp"),
        P("dp", "seq", "mp"),
        P("dp", "seq", "mp"),
        P("mp", ("dp", "seq")),
        P(),
        P(),
    )
    return jax.shard_map(
        local, mesh=mesh, in_specs=placed, out_specs=P(("dp", "seq", "mp"), None), check_vma=False
    )
```

time: 69 us -> 59.2 us (0.86)
  Pallas kernels: 64 us -> 58.1 us
  local copies, waits for them, and re-layouts: 4.46 us -> 0.71 us
    pallas_call x1, Pallas kernels: 64 us -> 58.1 us  [local(): pl.pallas_call(kernel, out_shape=jax.ShapeDtypeStruct((16, 32 * columns),...]
    unnamed x13 -> x1, local copies, waits for them, and re-layouts: 3.56 us -> 0.71 us
    reshape x1 -> x0, local copies, waits for them, and re-layouts: 0.89 us -> none  [local(): kv = resp_kv.reshape(slots, cap, 2 * HD)]
where the time goes in v2:
time: 59.2 us; the launch traced here: 58.8 us
  Pallas kernels  58.1 us (98%)
  local copies, waits for them, and re-layouts  0.71 us (1%)
    pallas_call x1, Pallas kernels, local(): pl.pallas_call(kernel, out_shape=jax.ShapeDtypeStruct((16, 32 * columns),...  58.1 us

profile of v2, /device:TPU:8, one launch (start us, length us, event | category | flops | bytes accessed | tf_op | source)
XLA Modules:
  0.0 58.8 jit_solution(16501021686360042812)
XLA Ops:
  0.0 58.1 %attend_project.1 = bf16[16,8192]{1,0:T(8,128)(2,1)S(1)} custom-call(s32[4,32]{1,0:T(4,128)} %bitcast.2, s32[4,32]{1,0:T(4,128)} %bitcast.3, bf16[1,4,32,1024]{3,2,1,0:T(8,128)(2,1)} %q_hbm.1, bf16[1,4,32,2,128]{4,3,2,1,0:T(2,128)(2,1)} %kv_hbm.1, bf16[1,128,128]{2,1,0:T(8,128)(2,1)} %k_hbm.1, bf16[1,128,128]{2,1,0:T(8,128)(2,1)} %v_hbm.1, ...), custom_call_target="tpu_custom_call" | custom-call | flops 2700000000 | bytes 2000000 | tf_op jit(solution)/shard_map/attend_project/pallas_call | solution.py:450
  58.1 0.7 %copy.9 = bf16[16,8192]{1,0:T(8,128)(2,1)} copy(bf16[16,8192]{1,0:T(8,128)(2,1)S(1)} %attend_project.1) | data formatting | bytes 524288

commit v3 on v2

--- a/solution.py
+++ b/solution.py
@@ -12,6 +12,7 @@
 Y_OFF = (0, 1, 3, 2)
 BATCHES = ((0, 1), (2, 3))
 GROUPS = ((0, 3), (3, 4))
+LAST = ((0, 1), (1, 2), (2, 3), (3, 4))
 
 
 class Ids:
@@ -35,23 +36,21 @@
 IDS = Ids()
 S_Q = IDS.take(4)
 S_K = IDS.take(4)
-S_V = IDS.take(4)
 S_KS = IDS.take(4)
-S_VS = IDS.take(4)
 S_WSIB = IDS.take(1)
 S_WSWAP = IDS.take(2)
 S_WRING = IDS.take(2, 2, 2)
 S_WSHARE = IDS.take(2, 5)
 S_A = IDS.take(len(BATCHES), 4, 2)
-S_R = IDS.take(4, len(GROUPS), 4)
-S_G = IDS.take(len(GROUPS), 8)
+S_R = IDS.take(4, 4, 4)
+S_G = IDS.take(4, 8)
 N_SEM = IDS.n
 
 
 def kernel(
     prompt_hbm, length_hbm, q_hbm, kv_hbm, k_hbm, v_hbm, w_ref, out_ref,
     prompt_of, lengths, q_ref, kv_ref,
-    qs, qb, kb, vb, wb, ab, cs, rb, fs, gb, ss, rs, lsem,
+    qs, qb, kb, wb, ab, cs, rb, fs, gb, ss, rs, lsem,
 ):
     y = lax.axis_index("dp")
     seq = lax.axis_index("seq")
@@ -105,8 +104,8 @@
                 (length_hbm, lengths),
                 (q_hbm.at[0], q_ref),
                 (kv_hbm.at[0], kv_ref),
-                (k_hbm.at[0], kb.at[own_rows]),
-                (v_hbm.at[0], vb.at[own_rows]),
+                (k_hbm.at[0], kb.at[own_rows, 0:HD]),
+                (v_hbm.at[0], kb.at[own_rows, HD : 2 * HD]),
             )
         )
     ]
@@ -121,12 +120,35 @@
 
     barrier = pltpu.get_barrier_semaphore()
     peers = [at_y(1), at_y(2), at_y(3), sibling, at_x(1), at_x(2), at_x(3)]
-    peers += [at_z(m) for m in range(1, 8)]
+    peers += [at_z(m) for m in (4, 3, 5, 2, 6, 1, 7)]
     peers.append((y, zh * 2 + 1 - c, x * 2 + 1 - zl))
     for peer in peers:
         pl.semaphore_signal(barrier, inc=1, device_id=peer, device_id_type=MESH)
 
-    for cp in fetches:
+    for cp in fetches[4:]:
+        cp.wait()
+    pl.semaphore_wait(barrier, len(peers))
+
+    swaps = []
+    for j in range(2):
+        rows = pl.ds(j * half_k, half_k)
+        swaps.append(
+            copy(
+                w_ref.at[rows], wb.at[y, zl, rows], S_WSWAP(j), S_WSWAP(0),
+                (y, zh * 2 + j, x * 2 + 1 - zl),
+            )
+        )
+
+    def swap_start():
+        @pl.when(jnp.logical_not(keeps))
+        def _():
+            for cp in swaps:
+                cp.start()
+
+    for m in (2, 1, 3):
+        send(kb.at[own_rows], kb.at[own_rows], S_K(m), at_z(2 * m))
+    send(kb.at[own_rows], kb.at[own_rows], S_KS(0), sibling)
+    for cp in fetches[:4]:
         cp.wait()
     source = y * 8 + seq
     for k in range(4):
@@ -140,16 +162,8 @@
         to[at, :, width : width + HD] = pair[:, 0, :]
         to[at, :, width + HD : width + 2 * HD] = pair[:, 1, :]
 
-    pl.semaphore_wait(barrier, len(peers))
-
-    for m in (2, 1, 3):
-        send(kb.at[own_rows], kb.at[own_rows], S_K(m), at_z(2 * m))
     for k in (2, 1, 3):
         send(qs.at[k], qb.at[y], S_Q(k), at_y(k))
-    for m in (2, 1, 3):
-        send(vb.at[own_rows], vb.at[own_rows], S_V(m), at_z(2 * m))
-    send(kb.at[own_rows], kb.at[own_rows], S_KS(0), sibling)
-    send(vb.at[own_rows], vb.at[own_rows], S_VS(0), sibling)
 
     w_sib = copy(w_ref, wb.at[y, zl], S_WSIB(0), S_WSIB(0), sibling)
 
@@ -217,32 +231,15 @@
             w_shared(r, 3)
             w_shared(r, 4)
 
-    def forward(ref, first, then):
+    def k_forward():
         for m in (1, 3, 2):
             block = rows_of(lax.rem(zh + 4 - m, 4) * 2 + c)
-            arrived(ref.at[block], first(m))
-            send(ref.at[block], ref.at[block], then(m), sibling)
-
-    def shared(ref, then):
+            arrived(kb.at[block], S_K(m))
+            send(kb.at[block], kb.at[block], S_KS(m), sibling)
+
+    def k_shared():
         for m in range(4):
-            block = rows_of(lax.rem(zh + 4 - m, 4) * 2 + 1 - c)
-            arrived(ref.at[block], then(m))
-
-    swaps = []
-    for j in range(2):
-        rows = pl.ds(j * half_k, half_k)
-        swaps.append(
-            copy(
-                w_ref.at[rows], wb.at[y, zl, rows], S_WSWAP(j), S_WSWAP(0),
-                (y, zh * 2 + j, x * 2 + 1 - zl),
-            )
-        )
-
-    def swap_start():
-        @pl.when(jnp.logical_not(keeps))
-        def _():
-            for cp in swaps:
-                cp.start()
+            arrived(kb.at[rows_of(lax.rem(zh + 4 - m, 4) * 2 + 1 - c)], S_KS(m))
 
     def swap_end():
         arrived(wb.at[y, late, mine(c)], S_WSWAP(0))
@@ -263,7 +260,7 @@
         near_k = qb[d, :, width : width + HD]
         near_v = qb[d, :, width + HD : width + 2 * HD]
         nt = (((1,), (1,)), ((), ()))
-        far = lax.dot_general(q, kb[...], nt, preferred_element_type=jnp.float32)
+        far = lax.dot_general(q, kb[:, 0:HD], nt, preferred_element_type=jnp.float32)
         near = lax.dot_general(q, near_k, nt, preferred_element_type=jnp.float32)
         token = lax.rem(lax.broadcasted_iota(jnp.int32, near.shape, 0), cap)
         key = lax.broadcasted_iota(jnp.int32, near.shape, 1)
@@ -274,7 +271,7 @@
         far = jnp.exp2((far - top) * factor)
         near = jnp.exp2((near - top) * factor)
         total = jnp.sum(far, axis=1, keepdims=True) + jnp.sum(near, axis=1, keepdims=True)
-        result = jnp.dot(far.astype(jnp.bfloat16), vb[...], preferred_element_type=jnp.float32)
+        result = jnp.dot(far.astype(jnp.bfloat16), kb[:, HD : 2 * HD], preferred_element_type=jnp.float32)
         result = result + jnp.dot(
             near.astype(jnp.bfloat16), near_v, preferred_element_type=jnp.float32
         )
@@ -320,8 +317,11 @@
         off = (0, 3 - 2 * zl, 1 + 2 * zl, 2)[p]
         return lax.rem(zh + off, 4)
 
-    def cols(g):
-        first, last = GROUPS[g]
+    def span(p, g):
+        return (LAST if p == 3 else GROUPS)[g]
+
+    def cols(p, g):
+        first, last = span(p, g)
         return slice(first * columns, last * columns)
 
     def chunk_of(xx):
@@ -333,7 +333,7 @@
 
     def project(p, g):
         zz = pair(p)
-        for k in range(*GROUPS[g]):
+        for k in range(*span(p, g)):
             yk = lax.rem(y + Y_OFF[k], 4)
             value = jnp.dot(ab[zz, 0], wb[yk, 0], preferred_element_type=jnp.float32)
             value = value + jnp.dot(ab[zz, 1], wb[yk, 1], preferred_element_type=jnp.float32)
@@ -341,27 +341,27 @@
         for off in (2, 1, 3):
             rows = block_of(lax.rem(x + off, 4))
             send(
-                cs.at[p, rows, cols(g)], rb.at[p, off, :, cols(g)], S_R(p, g, off), at_x(off)
+                cs.at[p, rows, cols(p, g)], rb.at[p, off, :, cols(p, g)], S_R(p, g, off), at_x(off)
             )
 
     def reduce(p, g):
-        value = cs[p, block_of(x), cols(g)].astype(jnp.float32)
+        value = cs[p, block_of(x), cols(p, g)].astype(jnp.float32)
         for off in (1, 3, 2):
-            arrived(rb.at[p, off, :, cols(g)], S_R(p, g, off))
-            value = value + rb[p, off, :, cols(g)].astype(jnp.float32)
-        fs[p, :, cols(g)] = value.astype(jnp.bfloat16)
+            arrived(rb.at[p, off, :, cols(p, g)], S_R(p, g, off))
+            value = value + rb[p, off, :, cols(p, g)].astype(jnp.float32)
+        fs[p, :, cols(p, g)] = value.astype(jnp.bfloat16)
         zz = pair(p)
         for t in range(2):
             half = slice(t * half_cap, (t + 1) * half_cap)
             if p == 0:
                 @pl.when(zl == t)
                 def _():
-                    gb[z, :, cols(g)] = fs[p, half, cols(g)]
+                    gb[z, :, cols(p, g)] = fs[p, half, cols(p, g)]
         if p == 0:
             half = pl.ds(pl.multiple_of(late * half_cap, half_cap), half_cap)
             off = 1 + 6 * zl
             send(
-                fs.at[p, half, cols(g)], gb.at[z, :, cols(g)], S_G(g, 0) + off,
+                fs.at[p, half, cols(p, g)], gb.at[z, :, cols(p, g)], S_G(g, 0) + off,
                 (y, zz * 2 + c, x * 2 + late),
             )
         else:
@@ -369,44 +369,53 @@
                 half = slice(t * half_cap, (t + 1) * half_cap)
                 off = lax.rem(zz * 2 + t - z + 8, 8)
                 send(
-                    fs.at[p, half, cols(g)], gb.at[z, :, cols(g)], S_G(g, 0) + off,
+                    fs.at[p, half, cols(p, g)], gb.at[z, :, cols(p, g)], S_G(g, 0) + off,
                     (y, zz * 2 + c, x * 2 + t),
                 )
 
-    def collect(g):
-        for m in range(8):
-            zz = lax.rem(z + 8 - m, 8)
-            if m:
-                arrived(gb.at[zz, :, cols(g)], S_G(g, 0) + m)
-        for k in range(*GROUPS[g]):
-            yk = lax.rem(y + Y_OFF[k], 4)
-            for zz in range(8):
-                place = pl.ds(pl.multiple_of((yk * 8 + zz) * columns, columns), columns)
-                out_ref[:, place] = gb[zz, :, k * columns : (k + 1) * columns]
+    def collect(p, g):
+        zz = lax.rem(zh + (0, 1, 3, 2)[p], 4) * 2
+        first, last = span(p, g)
+        for t in range(2):
+            src = zz + t
+            if p:
+                arrived(gb.at[src, :, cols(p, g)], S_G(g, 0) + lax.rem(z - src + 8, 8))
+            elif t == 0:
+                partner = z + 1 - 2 * zl
+                off = 7 - 6 * zl
+                arrived(gb.at[partner, :, cols(p, g)], S_G(g, 0) + off)
+        for t in range(2):
+            src = zz + t
+            for k in range(first, last):
+                yk = lax.rem(y + Y_OFF[k], 4)
+                place = pl.ds(pl.multiple_of((yk * 8 + src) * columns, columns), columns)
+                out_ref[:, place] = gb[src, :, k * columns : (k + 1) * columns]
+
+    def drain(keep=0):
+        while len(pending) > keep:
+            pending.pop(0).wait_send()
 
     batches = range(len(BATCHES))
     w_start(0, zl)
     swap_start()
-    forward(kb, S_K, S_KS)
-    forward(vb, S_V, S_VS)
-    shared(kb, S_KS)
-    shared(vb, S_VS)
-    for b in batches:
+    k_forward()
+    k_shared()
+    a_start(0)
+    swap_end()
+    for b in batches[1:]:
         a_start(b)
-    swap_end()
     for b in batches:
         a_relay(b, 1)
     w_relay(0, zl)
-    for b in batches:
+    a_relay(0, 2)
+    w_relay(1, late)
+    for b in batches[1:]:
         a_relay(b, 2)
-    w_relay(1, late)
     w_near()
     project(0, 0)
     project(1, 0)
     for b in batches:
         a_relay(b, 3)
-    reduce(0, 0)
-    reduce(1, 0)
     project(2, 0)
     w_finish(0, zl)
     w_finish(1, late)
@@ -414,21 +423,27 @@
     project(0, 1)
     project(1, 1)
     project(2, 1)
-    reduce(2, 0)
+    reduce(0, 0)
+    reduce(1, 0)
+    drain(18)
     for b in batches:
         a_last(b)
-    project(3, 0)
-    project(3, 1)
+    for g in range(len(LAST)):
+        project(3, g)
     reduce(0, 1)
     reduce(1, 1)
+    reduce(2, 0)
     reduce(2, 1)
-    reduce(3, 0)
-    reduce(3, 1)
-    collect(0)
-    collect(1)
-
-    for cp in pending:
-        cp.wait_send()
+    for g in range(len(LAST)):
+        reduce(3, g)
+    for p in range(3):
+        for g in range(len(GROUPS)):
+            collect(p, g)
+    drain(8)
+    for g in range(len(LAST)):
+        collect(3, g)
+
+    drain()
 
     @pl.when(keeps)
     def _():
@@ -459,8 +474,7 @@
             pltpu.VMEM((slots, cap, 2, HD), bf),
             pltpu.VMEM((4, cap, packed), bf),
             pltpu.VMEM((4, cap, packed), bf),
-            pltpu.VMEM((8 * tokens, HD), bf),
-            pltpu.VMEM((8 * tokens, HD), bf),
+            pltpu.VMEM((8 * tokens, 2 * HD), bf),
             pltpu.VMEM((4, 2, k_rows, columns), bf),
             pltpu.VMEM((4, 2, 4 * cap, width), bf),
             pltpu.VMEM((4, 4 * cap, 4 * columns), bf),

time: 59.2 us -> 56.8 us (0.959)
  Pallas kernels: 58.1 us -> 56 us
    pallas_call x1, Pallas kernels: 58.1 us -> 56 us  [local(): pl.pallas_call(kernel, out_shape=jax.ShapeDtypeStruct((16, 32 * columns),...]
where the time goes in v3:
time: 56.8 us; the launch traced here: 56.7 us
  Pallas kernels  56 us (99%)
  local copies, waits for them, and re-layouts  0.71 us (1%)
    pallas_call x1, Pallas kernels, local(): pl.pallas_call(kernel, out_shape=jax.ShapeDtypeStruct((16, 32 * columns),...  56 us

profile of v3, /device:TPU:8, one launch (start us, length us, event | category | flops | bytes accessed | tf_op | source)
XLA Modules:
  0.0 56.7 jit_solution(12464025779364228462)
XLA Ops:
  0.0 56.0 %attend_project.1 = bf16[16,8192]{1,0:T(8,128)(2,1)S(1)} custom-call(s32[4,32]{1,0:T(4,128)} %bitcast.2, s32[4,32]{1,0:T(4,128)} %bitcast.3, bf16[1,4,32,1024]{3,2,1,0:T(8,128)(2,1)} %q_hbm.1, bf16[1,4,32,2,128]{4,3,2,1,0:T(2,128)(2,1)} %kv_hbm.1, bf16[1,128,128]{2,1,0:T(8,128)(2,1)} %k_hbm.1, bf16[1,128,128]{2,1,0:T(8,128)(2,1)} %v_hbm.1, ...), custom_call_target="tpu_custom_call" | custom-call | flops 2700000000 | bytes 2000000 | tf_op jit(solution)/shard_map/attend_project/pallas_call | solution.py:465
  56.0 0.7 %copy.9 = bf16[16,8192]{1,0:T(8,128)(2,1)} copy(bf16[16,8192]{1,0:T(8,128)(2,1)S(1)} %attend_project.1) | data formatting | bytes 524288

commit v4 on v3

--- a/solution.py
+++ b/solution.py
@@ -127,27 +127,6 @@
 
     for cp in fetches[4:]:
         cp.wait()
-    pl.semaphore_wait(barrier, len(peers))
-
-    swaps = []
-    for j in range(2):
-        rows = pl.ds(j * half_k, half_k)
-        swaps.append(
-            copy(
-                w_ref.at[rows], wb.at[y, zl, rows], S_WSWAP(j), S_WSWAP(0),
-                (y, zh * 2 + j, x * 2 + 1 - zl),
-            )
-        )
-
-    def swap_start():
-        @pl.when(jnp.logical_not(keeps))
-        def _():
-            for cp in swaps:
-                cp.start()
-
-    for m in (2, 1, 3):
-        send(kb.at[own_rows], kb.at[own_rows], S_K(m), at_z(2 * m))
-    send(kb.at[own_rows], kb.at[own_rows], S_KS(0), sibling)
     for cp in fetches[:4]:
         cp.wait()
     source = y * 8 + seq
@@ -162,6 +141,27 @@
         to[at, :, width : width + HD] = pair[:, 0, :]
         to[at, :, width + HD : width + 2 * HD] = pair[:, 1, :]
 
+    pl.semaphore_wait(barrier, len(peers))
+
+    swaps = []
+    for j in range(2):
+        rows = pl.ds(j * half_k, half_k)
+        swaps.append(
+            copy(
+                w_ref.at[rows], wb.at[y, zl, rows], S_WSWAP(j), S_WSWAP(0),
+                (y, zh * 2 + j, x * 2 + 1 - zl),
+            )
+        )
+
+    def swap_start():
+        @pl.when(jnp.logical_not(keeps))
+        def _():
+            for cp in swaps:
+                cp.start()
+
+    for m in (2, 1, 3):
+        send(kb.at[own_rows], kb.at[own_rows], S_K(m), at_z(2 * m))
+    send(kb.at[own_rows], kb.at[own_rows], S_KS(0), sibling)
     for k in (2, 1, 3):
         send(qs.at[k], qb.at[y], S_Q(k), at_y(k))
 

time: 56.8 us -> 56.8 us (level)
  no operation moved by 1% of the time
where the time goes in v4:
time: 56.8 us; the launch traced here: 56.7 us
  Pallas kernels  56 us (99%)
  local copies, waits for them, and re-layouts  0.71 us (1%)
    pallas_call x1, Pallas kernels, local(): pl.pallas_call(kernel, out_shape=jax.ShapeDtypeStruct((16, 32 * columns),...  56 us

profile of v4, /device:TPU:8, one launch (start us, length us, event | category | flops | bytes accessed | tf_op | source)
XLA Modules:
  0.0 56.7 jit_solution(8947473366128872030)
XLA Ops:
  0.0 56.0 %attend_project.1 = bf16[16,8192]{1,0:T(8,128)(2,1)S(1)} custom-call(s32[4,32]{1,0:T(4,128)} %bitcast.2, s32[4,32]{1,0:T(4,128)} %bitcast.3, bf16[1,4,32,1024]{3,2,1,0:T(8,128)(2,1)} %q_hbm.1, bf16[1,4,32,2,128]{4,3,2,1,0:T(2,128)(2,1)} %kv_hbm.1, bf16[1,128,128]{2,1,0:T(8,128)(2,1)} %k_hbm.1, bf16[1,128,128]{2,1,0:T(8,128)(2,1)} %v_hbm.1, ...), custom_call_target="tpu_custom_call" | custom-call | flops 2700000000 | bytes 2000000 | tf_op jit(solution)/shard_map/attend_project/pallas_call | solution.py:465
  56.0 0.7 %copy.9 = bf16[16,8192]{1,0:T(8,128)(2,1)} copy(bf16[16,8192]{1,0:T(8,128)(2,1)S(1)} %attend_project.1) | data formatting | bytes 524288

commit v5 on v4

--- a/solution.py
+++ b/solution.py
@@ -404,9 +404,9 @@
     swap_end()
     for b in batches[1:]:
         a_start(b)
-    for b in batches:
-        a_relay(b, 1)
+    a_relay(0, 1)
     w_relay(0, zl)
+    a_relay(1, 1)
     a_relay(0, 2)
     w_relay(1, late)
     for b in batches[1:]:

time: 56.8 us -> 56.8 us (level)
  no operation moved by 1% of the time
where the time goes in v5:
time: 56.8 us; the launch traced here: 56.7 us
  Pallas kernels  56 us (99%)
  local copies, waits for them, and re-layouts  0.71 us (1%)
    pallas_call x1, Pallas kernels, local(): pl.pallas_call(kernel, out_shape=jax.ShapeDtypeStruct((16, 32 * columns),...  56 us

profile of v5, /device:TPU:8, one launch (start us, length us, event | category | flops | bytes accessed | tf_op | source)
XLA Modules:
  0.0 56.7 jit_solution(10582558252013247361)
XLA Ops:
  0.0 56.0 %attend_project.1 = bf16[16,8192]{1,0:T(8,128)(2,1)S(1)} custom-call(s32[4,32]{1,0:T(4,128)} %bitcast.2, s32[4,32]{1,0:T(4,128)} %bitcast.3, bf16[1,4,32,1024]{3,2,1,0:T(8,128)(2,1)} %q_hbm.1, bf16[1,4,32,2,128]{4,3,2,1,0:T(2,128)(2,1)} %kv_hbm.1, bf16[1,128,128]{2,1,0:T(8,128)(2,1)} %k_hbm.1, bf16[1,128,128]{2,1,0:T(8,128)(2,1)} %v_hbm.1, ...), custom_call_target="tpu_custom_call" | custom-call | flops 2700000000 | bytes 2000000 | tf_op jit(solution)/shard_map/attend_project/pallas_call | solution.py:465
  56.0 0.7 %copy.9 = bf16[16,8192]{1,0:T(8,128)(2,1)} copy(bf16[16,8192]{1,0:T(8,128)(2,1)S(1)} %attend_project.1) | data formatting | bytes 524288
